TPU v7x, 128 devices: a whole 4x4x4 slice. The times are simulated.
128 devices in a mesh: gx: 4 (over y), gy: 4 (over z_lo, core), gz: 8 (over x, z_hi).
Axes of the slice: x: 4, y: 4, z: 4 (z_hi: 2, z_lo: 2; z = z_hi * 2 + z_lo), core: 2. Of those that a mesh axis runs over, the one named last changes fastest.
Arguments:
- orbitals: float32 [16, 32, 128, 1024], P(None, 'gx', 'gy', 'gz'), may hold values from -9 to 9, as said below
- potential: float32 [32, 128, 1024], P('gx', 'gy', 'gz'), may hold values from -6 to 0
Outputs:
- filtered: float32 [16, 32, 128, 1024], P(None, 'gx', 'gy', 'gz')
- gram: float32 [16, 16], replicated
- projected: float32 [16, 16], replicated
Inputs may be any that keep to these rules, and one draw needn't show every extreme that they name: `orbitals`: real entries.
All inputs are finite; a program needn't handle non-finite values.
Results may differ from a plain program's by a relative error of at most 0.000075.
Values sent between devices are 32-bit elements; how exact they have to be, the bound alone decides.
A program may use at most 128 MiB of HBM per device.

v0:
```python
import jax
import jax.numpy as jnp
from jax import lax
from jax.sharding import PartitionSpec as P

coefs = (-205.0 / 72.0, 8.0 / 5.0, -1.0 / 5.0, 8.0 / 315.0, -1.0 / 560.0)
stencil_reach = 4
kinetic = -0.5 / 0.25
spread = 20.0
middle = 25.0
sigma_one = spread / (-6.0 - middle)
sigma_two = 1.0 / (2.0 / sigma_one - sigma_one)


def padded_2(block, sides, width):
    for axis, dim in sides:
        count = lax.axis_size(axis)
        forward = [(i, i + 1) for i in range(count - 1)]
        forward.append((count - 1, 0))
        backward = [(target, source) for source, target in forward]
        low = lax.ppermute(
            lax.slice_in_dim(block, block.shape[dim] - width, None, axis=dim), axis, forward
        )
        high = lax.ppermute(lax.slice_in_dim(block, 0, width, axis=dim), axis, backward)
        block = jnp.concatenate([low, block, high], axis=dim)
    return block


def apply_stencil(padded, potential, size_x, size_y, size_z):
    center = padded[
        :,
        stencil_reach : stencil_reach + size_x,
        stencil_reach : stencil_reach + size_y,
        stencil_reach : stencil_reach + size_z,
    ]
    total = 3.0 * coefs[0] * center
    for step in range(1, stencil_reach + 1):
        along_x = (
            padded[
                :,
                stencil_reach + step : stencil_reach + step + size_x,
                stencil_reach : stencil_reach + size_y,
                stencil_reach : stencil_reach + size_z,
            ]
            + padded[
                :,
                stencil_reach - step : stencil_reach - step + size_x,
                stencil_reach : stencil_reach + size_y,
                stencil_reach : stencil_reach + size_z,
            ]
        )
        along_y = (
            padded[
                :,
                stencil_reach : stencil_reach + size_x,
                stencil_reach + step : stencil_reach + step + size_y,
                stencil_reach : stencil_reach + size_z,
            ]
            + padded[
                :,
                stencil_reach : stencil_reach + size_x,
                stencil_reach - step : stencil_reach - step + size_y,
                stencil_reach : stencil_reach + size_z,
            ]
        )
        along_z = (
            padded[
                :,
                stencil_reach : stencil_reach + size_x,
                stencil_reach : stencil_reach + size_y,
                stencil_reach + step : stencil_reach + step + size_z,
            ]
            + padded[
                :,
                stencil_reach : stencil_reach + size_x,
                stencil_reach : stencil_reach + size_y,
                stencil_reach - step : stencil_reach - step + size_z,
            ]
        )
        total = total + coefs[step] * (along_x + along_y + along_z)
    return kinetic * total + potential[None] * center


def hamiltonian(field, potential):
    count, size_x, size_y, size_z = field.shape
    padded = padded_2(field, (("gx", 1), ("gy", 2), ("gz", 3)), 4)
    return apply_stencil(padded, potential, size_x, size_y, size_z)


def inner_rows(left, right):
    count = left.shape[0]
    return lax.dot_general(
        left.reshape(count, -1),
        right.reshape(count, -1),
        (((1,), (1,)), ((), ())),
        precision=lax.Precision.HIGHEST,
        preferred_element_type=jnp.float32,
    )


def shards(orbitals, potential):
    count, size_x, size_y, size_z = orbitals.shape
    cells_total = (
        size_x * size_y * size_z * lax.axis_size("gx") * lax.axis_size("gy") * lax.axis_size("gz")
    )
    first = sigma_one / spread * (hamiltonian(orbitals, potential) - middle * orbitals)
    filtered = (
        2.0 * sigma_two / spread * (hamiltonian(first, potential) - middle * first)
        - sigma_one * sigma_two * orbitals
    )
    correlation_part = inner_rows(filtered, filtered)
    padded = padded_2(filtered, (("gx", 1), ("gy", 2), ("gz", 3)), 4)
    image = apply_stencil(padded, potential, size_x, size_y, size_z)
    energy_part = inner_rows(filtered, image)
    gram, projected = lax.psum((correlation_part, energy_part), ("gx", "gy", "gz"))
    return (filtered, gram / cells_total, projected / cells_total)


def solution(mesh):
    placed = (P(None, "gx", "gy", "gz"), P("gx", "gy", "gz"))
    return jax.shard_map(
        shards,
        mesh=mesh,
        in_specs=placed,
        out_specs=(P(None, "gx", "gy", "gz"), P(), P()),
        check_vma=False,
    )
```

profile of v0, /device:TPU:1, one launch (start us, length us, event | category | flops | bytes accessed | tf_op | source)
XLA Modules:
  0.0 466.2 jit_solution(16324893196289675659)
XLA Ops:
  7.9 21.0 %collective-permute-done.1 = f32[16,4,32,128]{3,2,1,0:T(8,128)S(1)} collective-permute-done((f32[16,4,32,128]{3,2,1,0:T(8,128)S(1)}, f32[16,4,32,128]{3,2,1,0:T(8,128)S(1)}, u32[]{:S(2)}, u32[]{:S(2)}) %collective-permute-start.1) | collective-permute-done | bytes 1048608 | tf_op jit(solution)/shard_map/ppermute | solution.py:21
  35.6 12.6 %collective-permute-done.2 = f32[16,16,4,128]{3,1,2,0:T(8,128)S(1)} collective-permute-done((f32[16,16,4,128]{3,1,2,0:T(8,128)S(1)}, f32[16,16,4,128]{3,1,2,0:T(8,128)S(1)}, u32[]{:S(2)}, u32[]{:S(2)}) %collective-permute-start.2) | collective-permute-done | bytes 524320 | tf_op jit(solution)/shard_map/ppermute | solution.py:24
  49.2 5.8 %fusion.104 = (f32[16,16,40,4]{3,1,2,0:T(8,128)}, f32[16,16,40,4]{3,1,2,0:T(8,128)}) fusion(f32[16,16,40,128]{3,1,2,0:T(8,128)S(1)} %pad_maximum_fusion), kind=kLoop, calls=%fused_computation.207 | loop fusion | bytes 655360 | tf_op jit(solution)/shard_map/slice | solution.py:24
  69.7 5.9 %pad_maximum_fusion.3 = (f32[16,16,36,128]{3,1,2,0:T(8,128)}, f32[16,16,36,128]{3,1,2,0:T(8,128)}) fusion(f32[16,16,4,128]{3,1,2,0:T(8,128)} %copy-done.7, f32[16,4,32,128]{3,1,2,0:T(4,128)} %copy-done.2, f32[16,8,32,128]{3,1,2,0:T(8,128)S(1)} %get-tuple-element.36, f32[16,4,32,128]{3,1,2,0:T(4,128)S(1)} %copy.40, f32[16,16,4,128]{3,1,2,0:T(8,128)} %copy-done.10), kind=kLoop, calls=%fused_computation.33 | loop fusion | flops 7077888 | bytes 14680064 | tf_op jit(solution)/shard_map/concatenate | solution.py:25
  75.6 9.6 %collective-permute-done.5 = f32[16,16,40,4]{2,1,3,0:T(8,128)} collective-permute-done((f32[16,16,40,4]{2,1,3,0:T(8,128)}, f32[16,16,40,4]{2,1,3,0:T(8,128)}, u32[]{:S(2)}, u32[]{:S(2)}) %collective-permute-start.5) | collective-permute-done | bytes 163872 | tf_op jit(solution)/shard_map/ppermute | solution.py:21
  89.8 4.6 copy.46
  94.3 50.6 %broadcast_multiply_fusion = (f32[16,8,32,128]{3,1,2,0:T(8,128)S(1)}, f32[16,8,32,128]{3,1,2,0:T(8,128)}) fusion(f32[16,8,32,128]{3,1,2,0:T(8,128)} %copy-done.1, f32[8,32,128]{2,0,1:T(8,128)S(1)} %copy.49, f32[16,16,4,128]{3,1,2,0:T(8,128)} %copy-done.7, f32[16,4,32,128]{3,1,2,0:T(4,128)} %copy-done.2, f32[16,4,32,128]{3,1,2,0:T(4,128)S(1)} %copy.40, ...), kind=kLoop, calls=%fused_computation.190 | loop fusion | flops 41418752 | bytes 35061760 | tf_op jit(solution)/shard_map/mul | solution.py:106
  148.6 21.7 %collective-permute-done.7 = f32[16,4,32,128]{3,2,1,0:T(8,128)S(1)} collective-permute-done((f32[16,4,32,128]{3,2,1,0:T(8,128)S(1)}, f32[16,4,32,128]{3,2,1,0:T(8,128)S(1)}, u32[]{:S(2)}, u32[]{:S(2)}) %collective-permute-start.7) | collective-permute-done | bytes 1048608 | tf_op jit(solution)/shard_map/ppermute | solution.py:21
  174.3 10.5 %collective-permute-done.8 = f32[16,16,4,128]{3,1,2,0:T(8,128)S(1)} collective-permute-done((f32[16,16,4,128]{3,1,2,0:T(8,128)S(1)}, f32[16,16,4,128]{3,1,2,0:T(8,128)S(1)}, u32[]{:S(2)}, u32[]{:S(2)}) %collective-permute-start.8) | collective-permute-done | bytes 524320 | tf_op jit(solution)/shard_map/ppermute | solution.py:24
  186.7 5.8 %fusion.103 = (f32[16,16,40,4]{3,1,2,0:T(8,128)}, f32[16,16,40,4]{3,1,2,0:T(8,128)}) fusion(f32[16,16,40,128]{3,1,2,0:T(8,128)S(1)} %pad_maximum_fusion.1), kind=kLoop, calls=%fused_computation.206 | loop fusion | bytes 655360 | tf_op jit(solution)/shard_map/slice | solution.py:24
  201.0 4.5 copy.58
  207.8 5.9 %pad_maximum_fusion.4 = (f32[16,16,36,128]{3,1,2,0:T(8,128)}, f32[16,16,36,128]{3,1,2,0:T(8,128)}) fusion(f32[16,16,4,128]{3,1,2,0:T(8,128)} %copy-done.8, f32[16,4,32,128]{3,1,2,0:T(4,128)} %copy-done.3, f32[16,8,32,128]{3,1,2,0:T(8,128)S(1)} %get-tuple-element.11, f32[16,4,32,128]{3,1,2,0:T(4,128)S(1)} %copy.55, f32[16,16,4,128]{3,1,2,0:T(8,128)} %copy-done.11), kind=kLoop, calls=%fused_computation.35 | loop fusion | flops 7077888 | bytes 14680064 | tf_op jit(solution)/shard_map/concatenate | solution.py:25
  213.7 9.0 %collective-permute-done.11 = f32[16,16,40,4]{2,1,3,0:T(8,128)} collective-permute-done((f32[16,16,40,4]{2,1,3,0:T(8,128)}, f32[16,16,40,4]{2,1,3,0:T(8,128)}, u32[]{:S(2)}, u32[]{:S(2)}) %collective-permute-start.11) | collective-permute-done | bytes 163872 | tf_op jit(solution)/shard_map/ppermute | solution.py:21
  227.2 4.6 copy.59
  231.8 43.5 %fusion.35 = f32[16,8,32,128]{3,1,2,0:T(8,128)S(1)} fusion(f32[16,8,32,128]{3,1,2,0:T(8,128)} %copy-done, f32[16,4,32,128]{3,1,2,0:T(4,128)S(1)} %copy.55, f32[16,4,32,128]{3,1,2,0:T(4,128)} %copy-done.3, f32[16,16,40,4]{3,1,2,0:T(8,128)} %copy.61, f32[16,16,4,128]{3,1,2,0:T(8,128)} %copy-done.8, f32[16,16,4,128]{3,1,2,0:T(8,128)} %copy-done.11, ...), kind=kLoop, calls=%fused_computation.74 | loop fusion | flops 44564480 | bytes 28770304 | tf_op jit(solution)/shard_map/sub | solution.py:108
  278.9 20.9 %collective-permute-done.13 = f32[16,4,32,128]{3,2,1,0:T(8,128)S(1)} collective-permute-done((f32[16,4,32,128]{3,2,1,0:T(8,128)S(1)}, f32[16,4,32,128]{3,2,1,0:T(8,128)S(1)}, u32[]{:S(2)}, u32[]{:S(2)}) %collective-permute-start.13) | collective-permute-done | bytes 1048608 | tf_op jit(solution)/shard_map/ppermute | solution.py:21
  312.7 6.8 %collective-permute-done.14 = f32[16,16,4,128]{3,1,2,0:T(8,128)S(1)} collective-permute-done((f32[16,16,4,128]{3,1,2,0:T(8,128)S(1)}, f32[16,16,4,128]{3,1,2,0:T(8,128)S(1)}, u32[]{:S(2)}, u32[]{:S(2)}) %collective-permute-start.14) | collective-permute-done | bytes 524320 | tf_op jit(solution)/shard_map/ppermute | solution.py:24
  320.5 5.8 %fusion.102 = (f32[16,16,40,4]{3,1,2,0:T(8,128)}, f32[16,16,40,4]{3,1,2,0:T(8,128)}) fusion(f32[16,16,40,128]{3,1,2,0:T(8,128)S(1)} %pad_maximum_fusion.2), kind=kLoop, calls=%fused_computation.205 | loop fusion | bytes 655360 | tf_op jit(solution)/shard_map/slice | solution.py:24
  342.0 5.9 %pad_maximum_fusion.5 = (f32[16,16,36,128]{3,1,2,0:T(8,128)}, f32[16,16,36,128]{3,1,2,0:T(8,128)}) fusion(f32[16,16,4,128]{3,1,2,0:T(8,128)} %copy-done.9, f32[16,4,32,128]{3,1,2,0:T(4,128)} %copy-done.4, f32[16,8,32,128]{3,1,2,0:T(8,128)S(1)} %fusion.35, f32[16,4,32,128]{3,1,2,0:T(4,128)S(1)} %copy.69, f32[16,16,4,128]{3,1,2,0:T(8,128)} %copy-done.12), kind=kLoop, calls=%fused_computation.37 | loop fusion | flops 7077888 | bytes 14680064 | tf_op jit(solution)/shard_map/concatenate | solution.py:25
  347.9 9.5 %collective-permute-done.17 = f32[16,16,40,4]{2,1,3,0:T(8,128)} collective-permute-done((f32[16,16,40,4]{2,1,3,0:T(8,128)}, f32[16,16,40,4]{2,1,3,0:T(8,128)}, u32[]{:S(2)}, u32[]{:S(2)}) %collective-permute-start.17) | collective-permute-done | bytes 163872 | tf_op jit(solution)/shard_map/ppermute | solution.py:21
  362.0 4.6 copy.73
  366.6 27.5 %fusion.8 = f32[16,8,32,128]{3,1,2,0:T(8,128)S(1)} fusion(f32[16,8,32,128]{3,1,2,0:T(8,128)S(1)} %fusion.35, f32[16,4,32,128]{3,1,2,0:T(4,128)S(1)} %copy.69, f32[16,4,32,128]{3,1,2,0:T(4,128)} %copy-done.4, f32[16,16,40,4]{3,1,2,0:T(8,128)} %copy.75, f32[16,16,4,128]{3,1,2,0:T(8,128)} %copy-done.9, f32[16,16,4,128]{3,1,2,0:T(8,128)} %copy-done.12, ...), kind=kLoop, calls=%fused_computation.47 | loop fusion | flops 41943040 | bytes 24576000 | tf_op jit(solution)/shard_map/add | solution.py:81
  394.1 5.1 %fusion.96 = f32[16,16]{1,0:T(8,128)S(1)} fusion(f32[16,8,32,128]{3,1,2,0:T(8,128)S(1)} %fusion.8, f32[16,8,32,128]{3,1,2,0:T(8,128)S(1)} %fusion.35), kind=kOutput, calls=%fused_computation.189 | convolution fusion | flops 100663296 | bytes 4195328 | tf_op jit(solution)/shard_map/dot_general | solution.py:92
  399.2 66.2 %all-reduce = (f32[16,16]{1,0:T(8,128)S(1)}, f32[16,16]{1,0:T(8,128)S(1)}) all-reduce(f32[16,16]{1,0:T(8,128)S(1)} %fusion.93, f32[16,16]{1,0:T(8,128)S(1)} %fusion.96), channel_id=1, replica_groups=mesh['gx'=4,'gy'=4,'gz'=8] {'gx','gy','gz'}, use_global_device_ids=true, to_apply=%region_0.0 | all-reduce | flops 512 | bytes 4096 | tf_op jit(solution)/shard_map/psum | solution.py:115
  (89 shorter events, 97.1 us)
Async XLA Ops:
  0.6 5.6 %copy-start.6 = (f32[16,8,32,128]{3,2,1,0:T(8,128)S(1)}, f32[16,8,32,128]{3,2,1,0:T(8,128)}, u32[]{:S(2)}) copy-start(f32[16,8,32,128]{3,2,1,0:T(8,128)} %param.2) | copy-start | bytes 6291460
  2.5 26.4 %collective-permute-start.1 = (f32[16,4,32,128]{3,2,1,0:T(8,128)S(1)}, f32[16,4,32,128]{3,2,1,0:T(8,128)S(1)}, u32[]{:S(2)}, u32[]{:S(2)}) collective-permute-start(f32[16,4,32,128]{3,2,1,0:T(8,128)S(1)} %get-tuple-element.37), channel_id=1, source_target_pairs={{0,32},{32,64},{64,96},{96,0},{1,33},{33,65},{65,97},{97,1},{2,34}... | collective-permute-start | bytes 3145736 | tf_op jit(solution)/shard_map/ppermute | solution.py:21
  4.7 24.9 %collective-permute-start = (f32[16,4,32,128]{3,2,1,0:T(8,128)S(1)}, f32[16,4,32,128]{3,2,1,0:T(8,128)S(1)}, u32[]{:S(2)}, u32[]{:S(2)}) collective-permute-start(f32[16,4,32,128]{3,2,1,0:T(8,128)S(1)} %get-tuple-element.38), channel_id=1, source_target_pairs={{32,0},{64,32},{96,64},{0,96},{33,1},{65,33},{97,65},{1,97},{34,2}... | collective-permute-start | bytes 3145736 | tf_op jit(solution)/shard_map/ppermute | solution.py:24
  7.9 61.8 %copy-start.1 = (f32[16,8,32,128]{3,1,2,0:T(8,128)}, f32[16,8,32,128]{3,1,2,0:T(8,128)S(1)}, u32[]{:S(2)}) copy-start(f32[16,8,32,128]{3,1,2,0:T(8,128)S(1)} %get-tuple-element.36) | copy-start | bytes 6291460
  30.6 17.5 %copy-start.2 = (f32[16,4,32,128]{3,1,2,0:T(4,128)}, f32[16,4,32,128]{3,1,2,0:T(4,128)S(1)}, u32[]{:S(2)}) copy-start(f32[16,4,32,128]{3,1,2,0:T(4,128)S(1)} %get-tuple-element.40) | copy-start | bytes 3145732
  32.6 15.6 %collective-permute-start.2 = (f32[16,16,4,128]{3,1,2,0:T(8,128)S(1)}, f32[16,16,4,128]{3,1,2,0:T(8,128)S(1)}, u32[]{:S(2)}, u32[]{:S(2)}) collective-permute-start(f32[16,16,4,128]{3,1,2,0:T(8,128)S(1)} %get-tuple-element.30), channel_id=1, source_target_pairs={{8,0},{16,8},{24,16},{0,24},{9,1},{17,9},{25,17},{1,25},{10,2},{18... | collective-permute-start | bytes 1572872 | tf_op jit(solution)/shard_map/ppermute | solution.py:24
  34.0 14.2 %collective-permute-start.3 = (f32[16,16,4,128]{3,1,2,0:T(8,128)S(1)}, f32[16,16,4,128]{3,1,2,0:T(8,128)S(1)}, u32[]{:S(2)}, u32[]{:S(2)}) collective-permute-start(f32[16,16,4,128]{3,1,2,0:T(8,128)S(1)} %get-tuple-element.29), channel_id=1, source_target_pairs={{0,8},{8,16},{16,24},{24,0},{1,9},{9,17},{17,25},{25,1},{2,10},{10... | collective-permute-start | bytes 1572872 | tf_op jit(solution)/shard_map/ppermute | solution.py:21
  59.5 25.7 %collective-permute-start.5 = (f32[16,16,40,4]{2,1,3,0:T(8,128)}, f32[16,16,40,4]{2,1,3,0:T(8,128)}, u32[]{:S(2)}, u32[]{:S(2)}) collective-permute-start(f32[16,16,40,4]{2,1,3,0:T(8,128)} %copy.47), channel_id=1, source_target_pairs={{0,1},{1,2},{2,3},{3,4},{4,5},{5,6},{6,7},{7,0},{8,9},{9,10},{10,1... | collective-permute-start | bytes 491528 | tf_op jit(solution)/shard_map/ppermute | solution.py:21
  67.4 22.4 %collective-permute-start.4 = (f32[16,16,40,4]{2,1,3,0:T(8,128)}, f32[16,16,40,4]{2,1,3,0:T(8,128)}, u32[]{:S(2)}, u32[]{:S(2)}) collective-permute-start(f32[16,16,40,4]{2,1,3,0:T(8,128)} %copy.45), channel_id=1, source_target_pairs={{1,0},{2,1},{3,2},{4,3},{5,4},{6,5},{7,6},{0,7},{9,8},{10,9},{11,1... | collective-permute-start | bytes 491528 | tf_op jit(solution)/shard_map/ppermute | solution.py:24
  145.0 62.8 %copy-start = (f32[16,8,32,128]{3,1,2,0:T(8,128)}, f32[16,8,32,128]{3,1,2,0:T(8,128)S(1)}, u32[]{:S(2)}) copy-start(f32[16,8,32,128]{3,1,2,0:T(8,128)S(1)} %get-tuple-element.11) | copy-start | bytes 6291460
  145.6 24.6 %collective-permute-start.7 = (f32[16,4,32,128]{3,2,1,0:T(8,128)S(1)}, f32[16,4,32,128]{3,2,1,0:T(8,128)S(1)}, u32[]{:S(2)}, u32[]{:S(2)}) collective-permute-start(f32[16,4,32,128]{3,2,1,0:T(8,128)S(1)} %copy.54), channel_id=1, source_target_pairs={{0,32},{32,64},{64,96},{96,0},{1,33},{33,65},{65,97},{97,1},{2,34}... | collective-permute-start | bytes 3145736 | tf_op jit(solution)/shard_map/ppermute | solution.py:21
  146.3 24.7 %collective-permute-start.6 = (f32[16,4,32,128]{3,2,1,0:T(8,128)S(1)}, f32[16,4,32,128]{3,2,1,0:T(8,128)S(1)}, u32[]{:S(2)}, u32[]{:S(2)}) collective-permute-start(f32[16,4,32,128]{3,2,1,0:T(8,128)S(1)} %copy.52), channel_id=1, source_target_pairs={{32,0},{64,32},{96,64},{0,96},{33,1},{65,33},{97,65},{1,97},{34,2}... | collective-permute-start | bytes 3145736 | tf_op jit(solution)/shard_map/ppermute | solution.py:24
  171.7 14.1 %copy-start.3 = (f32[16,4,32,128]{3,1,2,0:T(4,128)}, f32[16,4,32,128]{3,1,2,0:T(4,128)S(1)}, u32[]{:S(2)}) copy-start(f32[16,4,32,128]{3,1,2,0:T(4,128)S(1)} %copy.53) | copy-start | bytes 3145732
  171.9 12.9 %collective-permute-start.8 = (f32[16,16,4,128]{3,1,2,0:T(8,128)S(1)}, f32[16,16,4,128]{3,1,2,0:T(8,128)S(1)}, u32[]{:S(2)}, u32[]{:S(2)}) collective-permute-start(f32[16,16,4,128]{3,1,2,0:T(8,128)S(1)} %get-tuple-element.26), channel_id=1, source_target_pairs={{8,0},{16,8},{24,16},{0,24},{9,1},{17,9},{25,17},{1,25},{10,2},{18... | collective-permute-start | bytes 1572872 | tf_op jit(solution)/shard_map/ppermute | solution.py:24
  174.2 11.6 %collective-permute-start.9 = (f32[16,16,4,128]{3,1,2,0:T(8,128)S(1)}, f32[16,16,4,128]{3,1,2,0:T(8,128)S(1)}, u32[]{:S(2)}, u32[]{:S(2)}) collective-permute-start(f32[16,16,4,128]{3,1,2,0:T(8,128)S(1)} %get-tuple-element.25), channel_id=1, source_target_pairs={{0,8},{8,16},{16,24},{24,0},{1,9},{9,17},{17,25},{25,1},{2,10},{10... | collective-permute-start | bytes 1572872 | tf_op jit(solution)/shard_map/ppermute | solution.py:21
  197.1 25.6 %collective-permute-start.11 = (f32[16,16,40,4]{2,1,3,0:T(8,128)}, f32[16,16,40,4]{2,1,3,0:T(8,128)}, u32[]{:S(2)}, u32[]{:S(2)}) collective-permute-start(f32[16,16,40,4]{2,1,3,0:T(8,128)} %copy.60), channel_id=1, source_target_pairs={{0,1},{1,2},{2,3},{3,4},{4,5},{5,6},{6,7},{7,0},{8,9},{9,10},{10,1... | collective-permute-start | bytes 491528 | tf_op jit(solution)/shard_map/ppermute | solution.py:21
  205.6 21.6 %collective-permute-start.10 = (f32[16,16,40,4]{2,1,3,0:T(8,128)}, f32[16,16,40,4]{2,1,3,0:T(8,128)}, u32[]{:S(2)}, u32[]{:S(2)}) collective-permute-start(f32[16,16,40,4]{2,1,3,0:T(8,128)} %copy.58), channel_id=1, source_target_pairs={{1,0},{2,1},{3,2},{4,3},{5,4},{6,5},{7,6},{0,7},{9,8},{10,9},{11,1... | collective-permute-start | bytes 491528 | tf_op jit(solution)/shard_map/ppermute | solution.py:24
  276.0 23.9 %collective-permute-start.13 = (f32[16,4,32,128]{3,2,1,0:T(8,128)S(1)}, f32[16,4,32,128]{3,2,1,0:T(8,128)S(1)}, u32[]{:S(2)}, u32[]{:S(2)}) collective-permute-start(f32[16,4,32,128]{3,2,1,0:T(8,128)S(1)} %copy.68), channel_id=1, source_target_pairs={{0,32},{32,64},{64,96},{96,0},{1,33},{33,65},{65,97},{97,1},{2,34}... | collective-permute-start | bytes 3145736 | tf_op jit(solution)/shard_map/ppermute | solution.py:21
  276.2 24.4 %collective-permute-start.12 = (f32[16,4,32,128]{3,2,1,0:T(8,128)S(1)}, f32[16,4,32,128]{3,2,1,0:T(8,128)S(1)}, u32[]{:S(2)}, u32[]{:S(2)}) collective-permute-start(f32[16,4,32,128]{3,2,1,0:T(8,128)S(1)} %copy.66), channel_id=1, source_target_pairs={{32,0},{64,32},{96,64},{0,96},{33,1},{65,33},{97,65},{1,97},{34,2}... | collective-permute-start | bytes 3145736 | tf_op jit(solution)/shard_map/ppermute | solution.py:24
  301.3 18.2 %copy-start.4 = (f32[16,4,32,128]{3,1,2,0:T(4,128)}, f32[16,4,32,128]{3,1,2,0:T(4,128)S(1)}, u32[]{:S(2)}) copy-start(f32[16,4,32,128]{3,1,2,0:T(4,128)S(1)} %copy.67) | copy-start | bytes 3145732
  301.5 18.0 %collective-permute-start.14 = (f32[16,16,4,128]{3,1,2,0:T(8,128)S(1)}, f32[16,16,4,128]{3,1,2,0:T(8,128)S(1)}, u32[]{:S(2)}, u32[]{:S(2)}) collective-permute-start(f32[16,16,4,128]{3,1,2,0:T(8,128)S(1)} %get-tuple-element.22), channel_id=1, source_target_pairs={{8,0},{16,8},{24,16},{0,24},{9,1},{17,9},{25,17},{1,25},{10,2},{18... | collective-permute-start | bytes 1572872 | tf_op jit(solution)/shard_map/ppermute | solution.py:24
  304.5 15.0 %collective-permute-start.15 = (f32[16,16,4,128]{3,1,2,0:T(8,128)S(1)}, f32[16,16,4,128]{3,1,2,0:T(8,128)S(1)}, u32[]{:S(2)}, u32[]{:S(2)}) collective-permute-start(f32[16,16,4,128]{3,1,2,0:T(8,128)S(1)} %get-tuple-element.21), channel_id=1, source_target_pairs={{0,8},{8,16},{16,24},{24,0},{1,9},{9,17},{17,25},{25,1},{2,10},{10... | collective-permute-start | bytes 1572872 | tf_op jit(solution)/shard_map/ppermute | solution.py:21
  330.8 26.6 %collective-permute-start.17 = (f32[16,16,40,4]{2,1,3,0:T(8,128)}, f32[16,16,40,4]{2,1,3,0:T(8,128)}, u32[]{:S(2)}, u32[]{:S(2)}) collective-permute-start(f32[16,16,40,4]{2,1,3,0:T(8,128)} %copy.74), channel_id=1, source_target_pairs={{0,1},{1,2},{2,3},{3,4},{4,5},{5,6},{6,7},{7,0},{8,9},{9,10},{10,1... | collective-permute-start | bytes 491528 | tf_op jit(solution)/shard_map/ppermute | solution.py:21
  339.7 22.3 %collective-permute-start.16 = (f32[16,16,40,4]{2,1,3,0:T(8,128)}, f32[16,16,40,4]{2,1,3,0:T(8,128)}, u32[]{:S(2)}, u32[]{:S(2)}) collective-permute-start(f32[16,16,40,4]{2,1,3,0:T(8,128)} %copy.72), channel_id=1, source_target_pairs={{1,0},{2,1},{3,2},{4,3},{5,4},{6,5},{7,6},{0,7},{9,8},{10,9},{11,1... | collective-permute-start | bytes 491528 | tf_op jit(solution)/shard_map/ppermute | solution.py:24
  (8 other events, 13.7 us)
where the time goes:
time: 474 us; the launch traced here: 466 us
  other arithmetic  143 us (30%)
  waiting for transfers between devices  123 us (26%)
  local copies, waits for them, and re-layouts  85.2 us (18%)
  blocking collectives  66.2 us (14%)
  starting transfers between devices  38.9 us (8%)
  matrix products  8.7 us (2%)
    ppermute x9, waiting for transfers between devices, padded_2(): lax.ppermute(lax.slice_in_dim(block, block.shape[dim] - width, None, axis...  92.7 us
    psum x1, blocking collectives, shards(): lax.psum((correlation_part, energy_part), ('gx', 'gy', 'gz'))  66.2 us
    mul x1, other arithmetic, shards(): sigma_one / spread * (hamiltonian(orbitals, potential) - middle * orbitals)  50.6 us
    sub x1, other arithmetic, shards(): 2.0 * sigma_two / spread * (hamiltonian(first, potential) - middle * first)  43.5 us
    slice x10, local copies, waits for them, and re-layouts, padded_2(): lax.slice_in_dim(block, 0, width, axis=dim)  32.2 us
    ppermute x9, waiting for transfers between devices, padded_2(): lax.ppermute(lax.slice_in_dim(block, 0, width, axis=dim), axis, backward)  30 us
    add x1, other arithmetic, apply_stencil(): return kinetic * total + potential[None] * center  27.5 us
    concatenate x9, other arithmetic, padded_2(): block = jnp.concatenate([low, block, high], axis=dim)  21.1 us
  transfers between devices with their start and end apart: 18, of which 10 were waited for; matrix products, arithmetic and copies ran while one was open for 12% of the time, Pallas kernels for 0%

commit v1 on v0

v1 whole, which is shorter than its diff:
```python
import functools

import jax
import jax.numpy as jnp
import ml_dtypes
import numpy as np
from jax import lax
from jax.experimental import pallas as pl
from jax.experimental.pallas import tpu as pltpu
from jax.sharding import PartitionSpec as P

MESH = pl.DeviceIdType.MESH
f32, bf16 = jnp.float32, jnp.bfloat16

coefs = (-205.0 / 72.0, 8.0 / 5.0, -1.0 / 5.0, 8.0 / 315.0, -1.0 / 560.0)
reach = 4
kinetic = -0.5 / 0.25
spread = 20.0
middle = 25.0
sigma_one = spread / (-6.0 - middle)
sigma_two = 1.0 / (2.0 / sigma_one - sigma_one)

axes = ("gx", "gy", "gz")
count, size_x, size_y, size_z = 16, 8, 32, 128
pairs = count // 2
cells = size_x * size_y
half = size_y // 2


def two_parts(matrix):
    high = matrix.astype(ml_dtypes.bfloat16)
    low = (matrix - high.astype(np.float64)).astype(ml_dtypes.bfloat16)
    return high, low


def weight(distance):
    return kinetic * coefs[abs(distance)] if 1 <= abs(distance) <= reach else 0.0


def constants():
    along_y = np.zeros((cells, cells))
    faces_y = np.zeros((cells, 2 * size_x * reach))
    for x in range(size_x):
        for y in range(size_y):
            for other in range(size_y):
                along_y[x * size_y + y, x * size_y + other] = weight(other - y)
            for r in range(reach):
                faces_y[x * size_y + y, x * reach + r] = weight(r - reach - y)
                faces_y[x * size_y + y, (size_x + x) * reach + r] = weight(size_y + r - y)
    along_z = np.zeros((size_z, size_z))
    faces_z = np.zeros((4 * reach, 2 * size_z))
    for z in range(size_z):
        for other in range(size_z):
            along_z[other, z] = weight(other - z)
        for r in range(reach):
            for o in range(2):
                faces_z[o * reach + r, o * size_z + z] = weight(r - reach - z)
                faces_z[(2 + o) * reach + r, o * size_z + z] = weight(size_z + r - z)
    pick_z = np.zeros((4 * reach, 2 * size_z))
    for r in range(reach):
        for o in range(2):
            pick_z[o * reach + r, o * size_z + r] = 1.0
            pick_z[(2 + o) * reach + r, o * size_z + size_z - reach + r] = 1.0
    gather = np.zeros((256, 128))
    for j in range(count):
        gather[8 * j : 8 * j + 8, j] = 1.0
        gather[128 + 8 * j : 128 + 8 * j + 8, count + j] = 1.0
    yh, yl = two_parts(along_y)
    fh, fl = two_parts(faces_y)
    zh, zl = two_parts(along_z)
    ch, cl = two_parts(faces_z)
    return (
        np.concatenate([yh, yh, yl], axis=1),
        np.concatenate([fh, fh, fl], axis=1),
        np.concatenate([zh, zh, zl], axis=0),
        np.concatenate([ch, ch, cl], axis=0),
        np.concatenate([pick_z, pick_z], axis=1).astype(ml_dtypes.bfloat16),
        gather.astype(ml_dtypes.bfloat16),
    )


def split(value):
    high = value.astype(bf16)
    return high, (value - high.astype(f32)).astype(bf16)


def dot(left, right, dims=((1,), (0,))):
    return lax.dot_general(left, right, (dims, ((), ())), preferred_element_type=f32)


def kernel(
    scale,
    o_ref, v_ref, ay_ref, fy_ref, az_ref, cz_ref, pick_ref, gather_ref,
    out_ref, gram_ref, proj_ref,
    first_ref, image_ref, xlo, xhi, xlo3, xhi3, ylo, yhi, ysl, ysh, zr, zs, sum_x, sum_y, sum_z,
    send_sem, recv_sem, sum_send, sum_recv,
):
    sizes = {a: lax.axis_size(a) for a in axes}
    me = {a: lax.axis_index(a) for a in axes}
    right = {a: lax.rem(me[a] + 1, sizes[a]) for a in axes}
    left = {a: lax.rem(me[a] + sizes[a] - 1, sizes[a]) for a in axes}

    barrier = pltpu.get_barrier_semaphore()
    greeted = 0
    for a in axes:
        for step in range(1, sizes[a]):
            pl.semaphore_signal(
                barrier, inc=1, device_id={a: lax.rem(me[a] + step, sizes[a])}, device_id_type=MESH
            )
            greeted += 1
    pl.semaphore_wait(barrier, greeted)

    def remote(src, dst, e, way, c, device):
        return pltpu.make_async_remote_copy(
            src_ref=src, dst_ref=dst, send_sem=send_sem.at[e, way], recv_sem=recv_sem.at[e, way, c],
            device_id=device, device_id_type=MESH,
        )

    def x_copies(e, field, two, c):
        if e < 2:
            return (
                remote(field.at[two, 0:reach], xhi.at[e, two], e, 0, c, {"gx": left["gx"]}),
                remote(field.at[two, size_x - reach : size_x], xlo.at[e, two], e, 1, c, {"gx": right["gx"]}),
            )
        return (
            remote(field.at[two, 0:reach, 0:half], xhi3.at[two], e, 0, c, {"gx": left["gx"]}),
            remote(field.at[two, size_x - reach : size_x, half:size_y], xlo3.at[two], e, 1, c, {"gx": right["gx"]}),
        )

    def yz_copies(e, two, one, c):
        low, high = pl.ds(0, 2 * reach), pl.ds(2 * reach, 2 * reach)
        return (
            remote(ysl.at[e, two], yhi.at[e, two], e, 2, c, {"gy": left["gy"]}),
            remote(ysh.at[e, two], ylo.at[e, two], e, 3, c, {"gy": right["gy"]}),
            remote(zs.at[e, one, low], zr.at[e, one, high], e, 4, c, {"gz": left["gz"]}),
            remote(zs.at[e, one, high], zr.at[e, one, low], e, 5, c, {"gz": right["gz"]}),
        )

    def pair(c):
        return pl.ds(2 * c, 2)

    def rows(ref, o):
        return ref[o].reshape(cells, size_z)

    def pack_send(e, field, c):
        for i in range(2):
            o = 2 * c + i
            for x in range(size_x):
                ysl[e, o, x * reach : (x + 1) * reach, :] = field[o, x, 0:reach, :]
                ysh[e, o, x * reach : (x + 1) * reach, :] = field[o, x, size_y - reach : size_y, :]
        h0, l0 = split(rows(field, 2 * c))
        h1, l1 = split(rows(field, 2 * c + 1))
        zs[e, c] = dot(pick_ref[...], jnp.concatenate([h0, h1, l0, l1], axis=1), ((1,), (1,)))
        for copy in yz_copies(e, pair(c), c, c):
            copy.start()

    def inner_yz(field, c):
        h0, l0 = split(rows(field, 2 * c))
        h1, l1 = split(rows(field, 2 * c + 1))
        high, low = jnp.concatenate([h0, h1], axis=1), jnp.concatenate([l0, l1], axis=1)
        y_part = dot(ay_ref[...], jnp.concatenate([high, low, high], axis=0))
        z_part = dot(
            jnp.concatenate(
                [jnp.concatenate([h0, l0, h0], axis=1), jnp.concatenate([h1, l1, h1], axis=1)], axis=0
            ),
            az_ref[...],
        )
        return y_part, z_part

    def faces_yz(e, c):
        around = jnp.concatenate(
            [jnp.concatenate([ylo[e, 2 * c + i], yhi[e, 2 * c + i]], axis=0) for i in range(2)], axis=1
        )
        high, low = split(around)
        y_part = dot(fy_ref[...], jnp.concatenate([high, low, high], axis=0))
        around = zr[e, c]
        high = around.astype(bf16).astype(f32)
        turned = jnp.concatenate([high, around - high, high], axis=0).T.astype(bf16)
        return y_part + dot(turned, cz_ref[...])

    def along_x(get, x):
        total = None
        for k in range(1, reach + 1):
            near = [v for v in (get(x - k), get(x + k)) if v is not None]
            if near:
                term = (near[0] if len(near) == 1 else near[0] + near[1]) * weight(k)
                total = term if total is None else total + term
        return total

    def hamiltonian(e, field, c, shift, write):
        y_part, z_part = inner_yz(field, c)
        around = None if e is None else faces_yz(e, c)
        for i in range(2):
            o = 2 * c + i

            def get(x):
                if x < 0:
                    return None if e is None else xlo[e, o, reach + x]
                if x >= size_x:
                    return None if e is None else xhi[e, o, x - size_x]
                return field[o, x]

            for x in range(size_x):
                block = slice(x * size_y, (x + 1) * size_y)
                lanes = slice(i * size_z, (i + 1) * size_z)
                value = y_part[block, lanes] + z_part[i * cells + x * size_y : i * cells + (x + 1) * size_y]
                if around is not None:
                    value = value + around[block, lanes]
                value = value + along_x(get, x)
                value = value + (v_ref[x] + (3.0 * kinetic * coefs[0] - shift)) * field[o, x]
                write(o, x, value)

    def wait_all(e, field, c):
        for copy in x_copies(e, field, pair(c), c) + yz_copies(e, pair(c), c, c):
            copy.wait_recv()

    def each(body):
        lax.fori_loop(0, pairs, lambda c, carry: (body(c), carry)[1], 0)

    def start_first(c):
        for copy in x_copies(0, o_ref, pair(c), c):
            copy.start()

    each(start_first)
    each(functools.partial(pack_send, 0, o_ref))

    def step_one(c):
        wait_all(0, o_ref, c)

        def write(o, x, value):
            first_ref[o, x] = value * (sigma_one / spread)

        hamiltonian(0, o_ref, c, middle, write)
        for copy in x_copies(1, first_ref, pair(c), c):
            copy.start()
        pack_send(1, first_ref, c)

    each(step_one)

    def step_two(c):
        wait_all(1, first_ref, c)

        def write(o, x, value):
            out_ref[o, x] = value * (2.0 * sigma_two / spread) - (sigma_one * sigma_two) * o_ref[o, x]

        hamiltonian(1, first_ref, c, middle, write)
        for copy in x_copies(2, out_ref, pair(c), c):
            copy.start()
        pack_send(2, out_ref, c)

        def write_image(o, x, value):
            image_ref[o, x] = value

        hamiltonian(None, out_ref, c, 0.0, write_image)

    each(step_two)

    def block(ref, x, tile):
        return split(ref[:, x, tile * 8 : (tile + 1) * 8, :].reshape(8 * count, size_z))

    def inner_block(x, tiles, with_gram):
        left, right = [], []
        for tile in tiles:
            fh, fl = block(out_ref, x, tile)
            gh, gl = block(image_ref, x, tile)
            left.append(jnp.concatenate([fh, fh, fl], axis=1))
            other = jnp.concatenate([gh, gl, gh], axis=1)
            if with_gram:
                other = jnp.concatenate([jnp.concatenate([fh, fl, fh], axis=1), other], axis=0)
            right.append(other)
        return dot(jnp.concatenate(left, axis=1), jnp.concatenate(right, axis=1), ((1,), (1,)))

    def with_gram(x, total):
        return total + inner_block(x, (0, 1), True) + inner_block(x, (2, 3), True)

    inner = lax.fori_loop(0, size_x, with_gram, jnp.zeros((8 * count, 16 * count), f32))

    def step_three(c):
        wait_all(2, out_ref, c)
        around = faces_yz(2, c)
        for i in range(2):
            o = 2 * c + i
            for x in range(size_x):
                value = around[x * size_y : (x + 1) * size_y, i * size_z : (i + 1) * size_z]
                if x < reach:
                    cross = along_x(lambda p: xlo3[o, reach + p] if p < 0 else None, x)
                    image_ref[o, x, 0:half] = value[0:half]
                    image_ref[o, x, half:size_y] = value[half:size_y] + 2.0 * cross
                else:
                    cross = along_x(lambda p: xhi3[o, p - size_x] if p >= size_x else None, x)
                    image_ref[o, x, 0:half] = value[0:half] + 2.0 * cross
                    image_ref[o, x, half:size_y] = value[half:size_y]

    each(step_three)

    def without_gram(x, total):
        return total + inner_block(x, (0, 1), False) + inner_block(x, (2, 3), False)

    outer = lax.fori_loop(0, size_x, without_gram, jnp.zeros((8 * count, 8 * count), f32))
    total = jnp.concatenate([inner[:, : 8 * count], inner[:, 8 * count :] + outer], axis=1)
    row = lax.broadcasted_iota(jnp.int32, total.shape, 0)
    lane = lax.broadcasted_iota(jnp.int32, total.shape, 1)
    total = jnp.where((row & 7) == (lane & 7), total, 0.0)
    total = total.reshape(count, 8, 16 * count).sum(axis=1)
    high, low = split(total)
    rest = (total - high.astype(f32) - low.astype(f32)).astype(bf16)
    share = dot(high, gather_ref[...]) + dot(low, gather_ref[...]) + dot(rest, gather_ref[...])

    for position, (a, slots) in enumerate(zip(axes, (sum_x, sum_y, sum_z))):
        slots[me[a]] = share

        def sum_copy(step):
            return pltpu.make_async_remote_copy(
                src_ref=slots.at[me[a]], dst_ref=slots.at[me[a]],
                send_sem=sum_send.at[position, step - 1], recv_sem=sum_recv.at[position, step - 1],
                device_id={a: lax.rem(me[a] + step, sizes[a])}, device_id_type=MESH,
            )

        copies = [sum_copy(step) for step in range(1, sizes[a])]
        for copy in copies:
            copy.start()
        for copy in copies:
            copy.wait()
        share = slots[0]
        for other in range(1, sizes[a]):
            share = share + slots[other]

    share = share * scale
    turned = share.T
    gram_ref[...] = share[:, 0:count]
    proj_ref[...] = 0.5 * (share[:, count : 2 * count] + turned[count : 2 * count, :])

    everything = pl.ds(0, count)
    for e, field in enumerate((o_ref, first_ref, out_ref)):
        for copy in x_copies(e, field, everything, 0) + yz_copies(e, everything, pl.ds(0, pairs), 0):
            copy.wait_send()


def shards(orbitals, potential):
    sizes = [lax.axis_size(a) for a in axes]
    total = cells * size_z * sizes[0] * sizes[1] * sizes[2]
    whole = pl.BlockSpec(memory_space=pltpu.VMEM)
    vmem = lambda *shape: pltpu.VMEM(shape, f32)
    return pl.pallas_call(
        functools.partial(kernel, 1.0 / total),
        out_shape=(
            jax.ShapeDtypeStruct(orbitals.shape, f32),
            jax.ShapeDtypeStruct((count, count), f32),
            jax.ShapeDtypeStruct((count, count), f32),
        ),
        in_specs=[whole] * 8,
        out_specs=(whole, whole, whole),
        scratch_shapes=[
            vmem(count, size_x, size_y, size_z),
            vmem(count, size_x, size_y, size_z),
            vmem(2, count, reach, size_y, size_z),
            vmem(2, count, reach, size_y, size_z),
            vmem(count, reach, half, size_z),
            vmem(count, reach, half, size_z),
            vmem(3, count, size_x * reach, size_z),
            vmem(3, count, size_x * reach, size_z),
            vmem(3, count, size_x * reach, size_z),
            vmem(3, count, size_x * reach, size_z),
            vmem(3, pairs, 4 * reach, cells),
            vmem(3, pairs, 4 * reach, cells),
            vmem(sizes[0], count, 128),
            vmem(sizes[1], count, 128),
            vmem(sizes[2], count, 128),
            pltpu.SemaphoreType.DMA((3, 6)),
            pltpu.SemaphoreType.DMA((3, 6, pairs)),
            pltpu.SemaphoreType.DMA((3, max(sizes))),
            pltpu.SemaphoreType.DMA((3, max(sizes))),
        ],
        compiler_params=pltpu.CompilerParams(
            collective_id=0, has_side_effects=True, vmem_limit_bytes=56 << 20
        ),
    )(orbitals, potential, *(jnp.asarray(c) for c in constants()))


def solution(mesh):
    placed = (P(None, "gx", "gy", "gz"), P("gx", "gy", "gz"))
    return jax.shard_map(
        shards,
        mesh=mesh,
        in_specs=placed,
        out_specs=(P(None, "gx", "gy", "gz"), P(), P()),
        check_vma=False,
    )
```

time: 474 us -> 89.5 us (0.19); the launches traced: 466 us -> 89.3 us
  other arithmetic: 143 us -> 0 us
  waiting for transfers between devices: 123 us -> 0 us
  Pallas kernels: 0 us -> 84.3 us
  local copies, waits for them, and re-layouts: 85.2 us -> 4.36 us
  blocking collectives: 66.2 us -> 0 us
  starting transfers between devices: 38.9 us -> 0 us
  matrix products: 8.7 us -> 0 us
    ppermute x18 -> x0, waiting for transfers between devices: 123 us -> none  [the longest x9 92.7 us: padded_2(): lax.ppermute(lax.slice_in_dim(block, block.shape[dim] - width, None, axis...]
    pallas_call x0 -> x1, Pallas kernels: none -> 84.3 us  [shards(): pl.pallas_call(functools.partial(kernel, 1.0 / total), out_shape=(jax.Sha...]
    psum x1 -> x0, blocking collectives: 66.2 us -> none  [shards(): lax.psum((correlation_part, energy_part), ('gx', 'gy', 'gz'))]
    mul x2 -> x0, other arithmetic: 50.7 us -> none  [the longest x1 50.6 us: shards(): sigma_one / spread * (hamiltonian(orbitals, potential) - middle * orbitals)]
    slice x16 -> x0, local copies, waits for them, and re-layouts: 48 us -> none  [the longest x10 32.2 us: padded_2(): lax.slice_in_dim(block, 0, width, axis=dim)]
    sub x1 -> x0, other arithmetic: 43.5 us -> none  [shards(): 2.0 * sigma_two / spread * (hamiltonian(first, potential) - middle * first)]
    ppermute x18 -> x0, starting transfers between devices: 38.9 us -> none  [the longest x9 20.2 us: padded_2(): lax.ppermute(lax.slice_in_dim(block, 0, width, axis=dim), axis, backward)]
    ppermute x11 -> x0, local copies, waits for them, and re-layouts: 30.9 us -> none  [the longest x6 15.7 us: padded_2(): lax.ppermute(lax.slice_in_dim(block, block.shape[dim] - width, None, axis...]
  transfers between devices with their start and end apart: 18 -> 0, of which waited for: 10 -> 0; matrix products, arithmetic and copies ran while one was open for 12% -> 0% of each run, Pallas kernels for 0% -> 0%
where the time goes in v1:
time: 89.5 us; the launch traced here: 89.3 us
  Pallas kernels  84.3 us (94%)
  local copies, waits for them, and re-layouts  4.36 us (5%)
    pallas_call x1, Pallas kernels, shards(): pl.pallas_call(functools.partial(kernel, 1.0 / total), out_shape=(jax.Sha...  84.3 us
    unnamed x7, local copies, waits for them, and re-layouts  4.36 us

profile of v1, /device:TPU:1, one launch (start us, length us, event | category | flops | bytes accessed | tf_op | source)
XLA Modules:
  0.0 89.3 jit_solution(3432661212477717887)
XLA Ops:
  0.6 84.3 %shard_map.103 = (f32[16,8,32,128]{3,2,1,0:T(8,128)}, f32[16,16]{1,0:T(8,128)}, f32[16,16]{1,0:T(8,128)}) custom-call(f32[16,8,32,128]{3,2,1,0:T(8,128)} %o_ref.1, f32[8,32,128]{2,1,0:T(8,128)} %v_ref.1, bf16[256,768]{1,0:T(8,128)(2,1)} %constant.12.clone.ay_ref, bf16[256,192]{1,0:T(8,128)(2,1)} %constant.13.clone.fy_ref, ...), custom_call_target="tpu_custom_call" | custom-call | tf_op jit(solution)/shard_map/pallas_call | solution.py:344
  85.0 0.0 copy-start.1
  85.0 0.0 copy-start
  85.0 3.2 %copy.14 = f32[16,8,32,128]{3,2,1,0:T(8,128)} copy(f32[16,8,32,128]{3,2,1,0:T(8,128)} %get-tuple-element.6) | data formatting | bytes 4194304
  88.1 0.0 copy-done.1
  88.1 0.6 copy.15
  88.7 0.0 copy-done
  88.7 0.6 copy.16
Async XLA Ops:
  85.0 3.2 %copy-start.1 = (f32[16,16]{1,0:T(8,128)S(1)}, f32[16,16]{1,0:T(8,128)}, u32[]{:S(2)}) copy-start(f32[16,16]{1,0:T(8,128)} %get-tuple-element.7) | copy-start | bytes 3076
  85.0 3.8 %copy-start = (f32[16,16]{1,0:T(8,128)S(1)}, f32[16,16]{1,0:T(8,128)}, u32[]{:S(2)}) copy-start(f32[16,16]{1,0:T(8,128)} %get-tuple-element.8) | copy-start | bytes 3076

commit v2 on v1

--- a/solution.py
+++ b/solution.py
@@ -90,25 +90,46 @@
 
 def kernel(
     scale,
+    o_hbm, v_hbm, ay_hbm, fy_hbm, az_hbm, cz_hbm, pick_hbm, gather_hbm,
+    out_ref, gram_ref, proj_ref,
     o_ref, v_ref, ay_ref, fy_ref, az_ref, cz_ref, pick_ref, gather_ref,
-    out_ref, gram_ref, proj_ref,
-    first_ref, image_ref, xlo, xhi, xlo3, xhi3, ylo, yhi, ysl, ysh, zr, zs, sum_x, sum_y, sum_z,
-    send_sem, recv_sem, sum_send, sum_recv,
+    first_ref, image_ref, cross_ref, xlo, xhi, xlo3, xhi3, ylo, yhi, ysl, ysh, zr, zs, sum_one, sum_two,
+    load_sem, send_sem, recv_sem, sum_send, sum_recv,
 ):
+    loads = [
+        pltpu.make_async_copy(src, dst, load_sem.at[i])
+        for i, (src, dst) in enumerate((
+            (o_hbm, o_ref), (pick_hbm, pick_ref), (v_hbm, v_ref), (ay_hbm, ay_ref), (fy_hbm, fy_ref),
+            (az_hbm, az_ref), (cz_hbm, cz_ref), (gather_hbm, gather_ref),
+        ))
+    ]
+    for load in loads:
+        load.start()
     sizes = {a: lax.axis_size(a) for a in axes}
     me = {a: lax.axis_index(a) for a in axes}
     right = {a: lax.rem(me[a] + 1, sizes[a]) for a in axes}
     left = {a: lax.rem(me[a] + sizes[a] - 1, sizes[a]) for a in axes}
 
+    def device(x, y, z):
+        return (x * sizes["gy"] + y) * sizes["gz"] + z
+
+    inner_z, outer_z = lax.rem(me["gz"], 2), me["gz"] // 2
+    outer_size = sizes["gz"] // 2
+    near = [
+        device(me["gx"], lax.rem(me["gy"] + y, sizes["gy"]), outer_z * 2 + lax.rem(inner_z + z, 2))
+        for y in range(sizes["gy"]) for z in range(2) if y + z
+    ]
+    far = [
+        device(lax.rem(me["gx"] + x, sizes["gx"]), me["gy"], lax.rem(outer_z + z, outer_size) * 2 + inner_z)
+        for x in range(sizes["gx"]) for z in range(outer_size) if x + z
+    ]
+    beside = device(me["gx"], me["gy"], lax.rem(me["gz"] + sizes["gz"] + 2 * inner_z - 1, sizes["gz"]))
+
     barrier = pltpu.get_barrier_semaphore()
-    greeted = 0
-    for a in axes:
-        for step in range(1, sizes[a]):
-            pl.semaphore_signal(
-                barrier, inc=1, device_id={a: lax.rem(me[a] + step, sizes[a])}, device_id_type=MESH
-            )
-            greeted += 1
-    pl.semaphore_wait(barrier, greeted)
+    greeted = near + far + [beside]
+    for other in greeted:
+        pl.semaphore_signal(barrier, inc=1, device_id=other, device_id_type=pl.DeviceIdType.LOGICAL)
+    pl.semaphore_wait(barrier, len(greeted))
 
     def remote(src, dst, e, way, c, device):
         return pltpu.make_async_remote_copy(
@@ -210,22 +231,31 @@
                 value = value + (v_ref[x] + (3.0 * kinetic * coefs[0] - shift)) * field[o, x]
                 write(o, x, value)
 
-    def wait_all(e, field, c):
-        for copy in x_copies(e, field, pair(c), c) + yz_copies(e, pair(c), c, c):
+    def wait_x(e, field, c):
+        for copy in x_copies(e, field, pair(c), c):
+            copy.wait_recv()
+
+    def wait_yz(e, c):
+        for copy in yz_copies(e, pair(c), c, c):
             copy.wait_recv()
 
     def each(body):
         lax.fori_loop(0, pairs, lambda c, carry: (body(c), carry)[1], 0)
 
     def start_first(c):
-        for copy in x_copies(0, o_ref, pair(c), c):
+        for copy in x_copies(0, o_hbm, pair(c), c):
             copy.start()
 
     each(start_first)
+    for load in loads[:2]:
+        load.wait()
     each(functools.partial(pack_send, 0, o_ref))
+    for load in loads[2:]:
+        load.wait()
 
     def step_one(c):
-        wait_all(0, o_ref, c)
+        wait_yz(0, c)
+        wait_x(0, o_hbm, c)
 
         def write(o, x, value):
             first_ref[o, x] = value * (sigma_one / spread)
@@ -238,7 +268,8 @@
     each(step_one)
 
     def step_two(c):
-        wait_all(1, first_ref, c)
+        wait_yz(1, c)
+        wait_x(1, first_ref, c)
 
         def write(o, x, value):
             out_ref[o, x] = value * (2.0 * sigma_two / spread) - (sigma_one * sigma_two) * o_ref[o, x]
@@ -255,104 +286,137 @@
 
     each(step_two)
 
-    def block(ref, x, tile):
-        return split(ref[:, x, tile * 8 : (tile + 1) * 8, :].reshape(8 * count, size_z))
-
-    def inner_block(x, tiles, with_gram):
-        left, right = [], []
-        for tile in tiles:
-            fh, fl = block(out_ref, x, tile)
-            gh, gl = block(image_ref, x, tile)
-            left.append(jnp.concatenate([fh, fh, fl], axis=1))
-            other = jnp.concatenate([gh, gl, gh], axis=1)
-            if with_gram:
-                other = jnp.concatenate([jnp.concatenate([fh, fl, fh], axis=1), other], axis=0)
-            right.append(other)
-        return dot(jnp.concatenate(left, axis=1), jnp.concatenate(right, axis=1), ((1,), (1,)))
-
-    def with_gram(x, total):
-        return total + inner_block(x, (0, 1), True) + inner_block(x, (2, 3), True)
-
-    inner = lax.fori_loop(0, size_x, with_gram, jnp.zeros((8 * count, 16 * count), f32))
-
-    def step_three(c):
-        wait_all(2, out_ref, c)
+    def add_faces(c):
+        wait_yz(2, c)
         around = faces_yz(2, c)
         for i in range(2):
             o = 2 * c + i
             for x in range(size_x):
-                value = around[x * size_y : (x + 1) * size_y, i * size_z : (i + 1) * size_z]
-                if x < reach:
-                    cross = along_x(lambda p: xlo3[o, reach + p] if p < 0 else None, x)
-                    image_ref[o, x, 0:half] = value[0:half]
-                    image_ref[o, x, half:size_y] = value[half:size_y] + 2.0 * cross
-                else:
-                    cross = along_x(lambda p: xhi3[o, p - size_x] if p >= size_x else None, x)
-                    image_ref[o, x, 0:half] = value[0:half] + 2.0 * cross
-                    image_ref[o, x, half:size_y] = value[half:size_y]
-
-    each(step_three)
-
-    def without_gram(x, total):
-        return total + inner_block(x, (0, 1), False) + inner_block(x, (2, 3), False)
-
-    outer = lax.fori_loop(0, size_x, without_gram, jnp.zeros((8 * count, 8 * count), f32))
-    total = jnp.concatenate([inner[:, : 8 * count], inner[:, 8 * count :] + outer], axis=1)
-    row = lax.broadcasted_iota(jnp.int32, total.shape, 0)
-    lane = lax.broadcasted_iota(jnp.int32, total.shape, 1)
-    total = jnp.where((row & 7) == (lane & 7), total, 0.0)
-    total = total.reshape(count, 8, 16 * count).sum(axis=1)
-    high, low = split(total)
-    rest = (total - high.astype(f32) - low.astype(f32)).astype(bf16)
-    share = dot(high, gather_ref[...]) + dot(low, gather_ref[...]) + dot(rest, gather_ref[...])
-
-    for position, (a, slots) in enumerate(zip(axes, (sum_x, sum_y, sum_z))):
-        slots[me[a]] = share
-
-        def sum_copy(step):
+                image_ref[o, x] += around[x * size_y : (x + 1) * size_y, i * size_z : (i + 1) * size_z]
+
+    each(add_faces)
+
+    def block(ref, which, x, tile):
+        rows = ref[which, x, tile * 8 : (tile + 1) * 8, :]
+        return split(rows.reshape(8 * rows.shape[0], size_z))
+
+    everything = slice(0, count)
+
+    def left_parts(x, tile):
+        high, low = block(out_ref, everything, x, tile)
+        return jnp.concatenate([high, high, low], axis=1), jnp.concatenate([high, low, high], axis=1)
+
+    def right_parts(ref, which, x, tile):
+        high, low = block(ref, which, x, tile)
+        return jnp.concatenate([high, low, high], axis=1)
+
+    def rows_dot(left, right):
+        return dot(jnp.concatenate(left, axis=1), jnp.concatenate(right, axis=1), ((1,), (1,)))
+
+    def inner_block(x, total):
+        for tiles in ((0, 1), (2, 3)):
+            left, right = [], []
+            for tile in tiles:
+                one, other = left_parts(x, tile)
+                left.append(one)
+                right.append(jnp.concatenate([other, right_parts(image_ref, everything, x, tile)], axis=0))
+            total = total + rows_dot(left, right)
+        return total
+
+    def collect(total, offset):
+        row = lax.broadcasted_iota(jnp.int32, total.shape, 0)
+        lane = lax.broadcasted_iota(jnp.int32, total.shape, 1)
+        total = jnp.where((row & 7) == (lane & 7), total, 0.0)
+        total = total.reshape(count, 8, total.shape[1]).sum(axis=1)
+        high, low = split(total)
+        rest = (total - high.astype(f32) - low.astype(f32)).astype(bf16)
+        picked = dot(jnp.concatenate([high, low, rest], axis=0), gather_ref[offset : offset + total.shape[1], :])
+        return picked[0:count] + picked[count : 2 * count] + picked[2 * count :]
+
+    inner = lax.fori_loop(0, size_x, inner_block, jnp.zeros((8 * count, 16 * count), f32))
+    share = collect(inner, 0)
+
+    def add_cross(c):
+        wait_x(2, out_ref, c)
+        for i in range(2):
+            o = 2 * c + i
+            for x in range(reach):
+                cross_ref[o, x, 0:half] = 2.0 * along_x(
+                    lambda p: xhi3[o, p - size_x] if p >= size_x else None, size_x - reach + x
+                )
+                cross_ref[o, x, half:size_y] = 2.0 * along_x(lambda p: xlo3[o, reach + p] if p < 0 else None, x)
+
+    part = count // 2
+    for begin in range(0, count, part):
+        lax.fori_loop(begin // 2, (begin + part) // 2, lambda c, carry: (add_cross(c), carry)[1], 0)
+
+        def cross_block(x, total):
+            for tiles, layer in (((0, 1), x + size_x - reach), ((2, 3), x)):
+                left = [left_parts(layer, tile)[0] for tile in tiles]
+                right = [right_parts(cross_ref, slice(begin, begin + part), x, tile) for tile in tiles]
+                total = total + rows_dot(left, right)
+            return total
+
+        cross = lax.fori_loop(0, reach, cross_block, jnp.zeros((8 * count, 8 * part), f32))
+        share = share + collect(cross, 8 * count + 8 * begin)
+
+    stages = (
+        (near, sum_one, me["gy"] * 2 + inner_z),
+        (far, sum_two, me["gx"] * outer_size + outer_z),
+    )
+    sent = []
+    for position, (others, slots, mine) in enumerate(stages):
+        slots[mine] = share
+
+        def sum_copy(ref, other):
             return pltpu.make_async_remote_copy(
-                src_ref=slots.at[me[a]], dst_ref=slots.at[me[a]],
-                send_sem=sum_send.at[position, step - 1], recv_sem=sum_recv.at[position, step - 1],
-                device_id={a: lax.rem(me[a] + step, sizes[a])}, device_id_type=MESH,
+                src_ref=ref, dst_ref=ref, send_sem=sum_send.at[position], recv_sem=sum_recv.at[position],
+                device_id=other, device_id_type=pl.DeviceIdType.LOGICAL,
             )
 
-        copies = [sum_copy(step) for step in range(1, sizes[a])]
-        for copy in copies:
-            copy.start()
-        for copy in copies:
-            copy.wait()
-        share = slots[0]
-        for other in range(1, sizes[a]):
-            share = share + slots[other]
+        for other in others:
+            sum_copy(slots.at[mine], other).start()
+        arrived = sum_copy(slots.at[pl.ds(0, len(others))], others[0])
+        arrived.wait_recv()
+        sent.append(arrived)
+        shares = [slots[i] for i in range(len(others) + 1)]
+        while len(shares) > 1:
+            shares = [shares[i] + shares[i + 1] for i in range(0, len(shares), 2)]
+        share = shares[0]
 
     share = share * scale
     turned = share.T
     gram_ref[...] = share[:, 0:count]
     proj_ref[...] = 0.5 * (share[:, count : 2 * count] + turned[count : 2 * count, :])
 
-    everything = pl.ds(0, count)
-    for e, field in enumerate((o_ref, first_ref, out_ref)):
-        for copy in x_copies(e, field, everything, 0) + yz_copies(e, everything, pl.ds(0, pairs), 0):
+    whole = pl.ds(0, count)
+    for e, field in enumerate((o_hbm, first_ref, out_ref)):
+        for copy in x_copies(e, field, whole, 0) + yz_copies(e, whole, pl.ds(0, pairs), 0):
             copy.wait_send()
+    for copy in sent:
+        copy.wait_send()
 
 
 def shards(orbitals, potential):
     sizes = [lax.axis_size(a) for a in axes]
     total = cells * size_z * sizes[0] * sizes[1] * sizes[2]
     whole = pl.BlockSpec(memory_space=pltpu.VMEM)
+    operands = (orbitals, potential, *(jnp.asarray(c) for c in constants()))
     vmem = lambda *shape: pltpu.VMEM(shape, f32)
     return pl.pallas_call(
         functools.partial(kernel, 1.0 / total),
         out_shape=(
-            jax.ShapeDtypeStruct(orbitals.shape, f32),
-            jax.ShapeDtypeStruct((count, count), f32),
-            jax.ShapeDtypeStruct((count, count), f32),
+            vmem(*orbitals.shape),
+            vmem(count, count),
+            vmem(count, count),
         ),
-        in_specs=[whole] * 8,
+        in_specs=[pl.BlockSpec(memory_space=pltpu.HBM)] * len(operands),
         out_specs=(whole, whole, whole),
         scratch_shapes=[
+            *(pltpu.VMEM(x.shape, x.dtype) for x in operands),
             vmem(count, size_x, size_y, size_z),
             vmem(count, size_x, size_y, size_z),
+            vmem(count, reach, size_y, size_z),
             vmem(2, count, reach, size_y, size_z),
             vmem(2, count, reach, size_y, size_z),
             vmem(count, reach, half, size_z),
@@ -363,18 +427,18 @@
             vmem(3, count, size_x * reach, size_z),
             vmem(3, pairs, 4 * reach, cells),
             vmem(3, pairs, 4 * reach, cells),
-            vmem(sizes[0], count, 128),
-            vmem(sizes[1], count, 128),
-            vmem(sizes[2], count, 128),
+            vmem(sizes[1] * 2, count, 128),
+            vmem(sizes[0] * sizes[2] // 2, count, 128),
+            pltpu.SemaphoreType.DMA((len(operands),)),
             pltpu.SemaphoreType.DMA((3, 6)),
             pltpu.SemaphoreType.DMA((3, 6, pairs)),
-            pltpu.SemaphoreType.DMA((3, max(sizes))),
-            pltpu.SemaphoreType.DMA((3, max(sizes))),
+            pltpu.SemaphoreType.DMA((2,)),
+            pltpu.SemaphoreType.DMA((2,)),
         ],
         compiler_params=pltpu.CompilerParams(
-            collective_id=0, has_side_effects=True, vmem_limit_bytes=56 << 20
+            collective_id=0, has_side_effects=True, vmem_limit_bytes=48 << 20
         ),
-    )(orbitals, potential, *(jnp.asarray(c) for c in constants()))
+    )(*(pltpu.with_memory_space_constraint(x, pltpu.HBM) for x in operands))
 
 
 def solution(mesh):

time: 89.5 us -> 81.4 us (0.909)
  Pallas kernels: 84.3 us -> 78.1 us
  local copies, waits for them, and re-layouts: 4.36 us -> 2.52 us
    pallas_call x1, Pallas kernels: 84.3 us -> 78.1 us  [shards(): pl.pallas_call(functools.partial(kernel, 1.0 / total), out_shape=(vmem(*o...]
    unnamed x7 -> x3, local copies, waits for them, and re-layouts: 4.36 us -> 2.52 us
where the time goes in v2:
time: 81.4 us; the launch traced here: 81.3 us
  Pallas kernels  78.1 us (96%)
  local copies, waits for them, and re-layouts  2.52 us (3%)
    pallas_call x1, Pallas kernels, shards(): pl.pallas_call(functools.partial(kernel, 1.0 / total), out_shape=(vmem(*o...  78.1 us
    unnamed x3, local copies, waits for them, and re-layouts  2.52 us

profile of v2, /device:TPU:1, one launch (start us, length us, event | category | flops | bytes accessed | tf_op | source)
XLA Modules:
  0.0 81.3 jit_solution(12444877150222282774)
XLA Ops:
  0.6 78.1 %shard_map.103 = (f32[16,8,32,128]{3,2,1,0:T(8,128)S(1)}, f32[16,16]{1,0:T(8,128)S(1)}, f32[16,16]{1,0:T(8,128)S(1)}) custom-call(f32[16,8,32,128]{3,2,1,0:T(8,128)} %o_hbm.1, f32[8,32,128]{2,1,0:T(8,128)} %v_hbm.1, bf16[256,768]{1,0:T(8,128)(2,1)} %constant.12.clone.ay_hbm, bf16[256,192]{1,0:T(8,128)(2,1)} %constant.13.clone.fy_hbm, ...), custom_call_target="tpu_custom_call" | custom-call | tf_op jit(solution)/shard_map/pallas_call | solution.py:406
  78.8 1.3 %copy.14 = f32[16,8,32,128]{3,2,1,0:T(8,128)} copy(f32[16,8,32,128]{3,2,1,0:T(8,128)S(1)} %get-tuple-element.3) | data formatting | bytes 4194304
  80.1 0.6 copy.15
  80.7 0.6 copy.16

commit v3 on v2

--- a/solution.py
+++ b/solution.py
@@ -91,9 +91,9 @@
 def kernel(
     scale,
     o_hbm, v_hbm, ay_hbm, fy_hbm, az_hbm, cz_hbm, pick_hbm, gather_hbm,
-    out_ref, gram_ref, proj_ref,
+    out_ref, sum_ref,
     o_ref, v_ref, ay_ref, fy_ref, az_ref, cz_ref, pick_ref, gather_ref,
-    first_ref, image_ref, cross_ref, xlo, xhi, xlo3, xhi3, ylo, yhi, ysl, ysh, zr, zs, sum_one, sum_two,
+    first_ref, image_ref, xlo, xhi, xlo3, xhi3, ylo, yhi, ysl, ysh, zr, zs, sum_one, sum_two,
     load_sem, send_sem, recv_sem, sum_send, sum_recv,
 ):
     loads = [
@@ -115,13 +115,19 @@
 
     inner_z, outer_z = lax.rem(me["gz"], 2), me["gz"] // 2
     outer_size = sizes["gz"] // 2
+    def hops(steps, size):
+        return min(steps, size - steps)
+
     near = [
         device(me["gx"], lax.rem(me["gy"] + y, sizes["gy"]), outer_z * 2 + lax.rem(inner_z + z, 2))
-        for y in range(sizes["gy"]) for z in range(2) if y + z
+        for z in (1, 0) for y in sorted(range(sizes["gy"]), key=lambda y: -hops(y, sizes["gy"])) if y + z
     ]
     far = [
         device(lax.rem(me["gx"] + x, sizes["gx"]), me["gy"], lax.rem(outer_z + z, outer_size) * 2 + inner_z)
-        for x in range(sizes["gx"]) for z in range(outer_size) if x + z
+        for x, z in sorted(
+            ((x, z) for x in range(sizes["gx"]) for z in range(outer_size) if x + z),
+            key=lambda xz: -hops(xz[0], sizes["gx"]) - hops(xz[1], outer_size),
+        )
     ]
     beside = device(me["gx"], me["gy"], lax.rem(me["gz"] + sizes["gz"] + 2 * inner_z - 1, sizes["gz"]))
 
@@ -284,8 +290,6 @@
 
         hamiltonian(None, out_ref, c, 0.0, write_image)
 
-    each(step_two)
-
     def add_faces(c):
         wait_yz(2, c)
         around = faces_yz(2, c)
@@ -294,21 +298,16 @@
             for x in range(size_x):
                 image_ref[o, x] += around[x * size_y : (x + 1) * size_y, i * size_z : (i + 1) * size_z]
 
-    each(add_faces)
-
-    def block(ref, which, x, tile):
-        rows = ref[which, x, tile * 8 : (tile + 1) * 8, :]
-        return split(rows.reshape(8 * rows.shape[0], size_z))
-
-    everything = slice(0, count)
-
-    def left_parts(x, tile):
-        high, low = block(out_ref, everything, x, tile)
-        return jnp.concatenate([high, high, low], axis=1), jnp.concatenate([high, low, high], axis=1)
-
-    def right_parts(ref, which, x, tile):
-        high, low = block(ref, which, x, tile)
-        return jnp.concatenate([high, low, high], axis=1)
+    def step_two_and_faces(c):
+        step_two(c)
+        add_faces(c - 1)
+
+    step_two(0)
+    lax.fori_loop(1, pairs, lambda c, carry: (step_two_and_faces(c), carry)[1], 0)
+    add_faces(pairs - 1)
+
+    def block(ref, x, tile):
+        return split(ref[:, x, tile * 8 : (tile + 1) * 8, :].reshape(8 * count, size_z))
 
     def rows_dot(left, right):
         return dot(jnp.concatenate(left, axis=1), jnp.concatenate(right, axis=1), ((1,), (1,)))
@@ -317,48 +316,66 @@
         for tiles in ((0, 1), (2, 3)):
             left, right = [], []
             for tile in tiles:
-                one, other = left_parts(x, tile)
-                left.append(one)
-                right.append(jnp.concatenate([other, right_parts(image_ref, everything, x, tile)], axis=0))
+                high, low = block(out_ref, x, tile)
+                other_high, other_low = block(image_ref, x, tile)
+                left.append(jnp.concatenate([high, high, low], axis=1))
+                right.append(
+                    jnp.concatenate(
+                        [
+                            jnp.concatenate([high, low, high], axis=1),
+                            jnp.concatenate([other_high, other_low, other_high], axis=1),
+                        ],
+                        axis=0,
+                    )
+                )
             total = total + rows_dot(left, right)
         return total
 
-    def collect(total, offset):
+    def three_parts(value):
+        high, low = split(value)
+        rest = (value - high.astype(f32) - low.astype(f32)).astype(bf16)
+        return jnp.concatenate([high, low, rest], axis=0)
+
+    def added_up(parts, length):
+        return parts[0:length] + parts[length : 2 * length] + parts[2 * length :]
+
+    def collect(total):
         row = lax.broadcasted_iota(jnp.int32, total.shape, 0)
         lane = lax.broadcasted_iota(jnp.int32, total.shape, 1)
         total = jnp.where((row & 7) == (lane & 7), total, 0.0)
         total = total.reshape(count, 8, total.shape[1]).sum(axis=1)
-        high, low = split(total)
-        rest = (total - high.astype(f32) - low.astype(f32)).astype(bf16)
-        picked = dot(jnp.concatenate([high, low, rest], axis=0), gather_ref[offset : offset + total.shape[1], :])
-        return picked[0:count] + picked[count : 2 * count] + picked[2 * count :]
+        return added_up(dot(three_parts(total), gather_ref[...]), count)
 
     inner = lax.fori_loop(0, size_x, inner_block, jnp.zeros((8 * count, 16 * count), f32))
-    share = collect(inner, 0)
-
-    def add_cross(c):
+    share = collect(inner)
+
+    def add_cross(c, share):
         wait_x(2, out_ref, c)
-        for i in range(2):
-            o = 2 * c + i
-            for x in range(reach):
-                cross_ref[o, x, 0:half] = 2.0 * along_x(
-                    lambda p: xhi3[o, p - size_x] if p >= size_x else None, size_x - reach + x
-                )
-                cross_ref[o, x, half:size_y] = 2.0 * along_x(lambda p: xlo3[o, reach + p] if p < 0 else None, x)
-
-    part = count // 2
-    for begin in range(0, count, part):
-        lax.fori_loop(begin // 2, (begin + part) // 2, lambda c, carry: (add_cross(c), carry)[1], 0)
-
-        def cross_block(x, total):
-            for tiles, layer in (((0, 1), x + size_x - reach), ((2, 3), x)):
-                left = [left_parts(layer, tile)[0] for tile in tiles]
-                right = [right_parts(cross_ref, slice(begin, begin + part), x, tile) for tile in tiles]
-                total = total + rows_dot(left, right)
-            return total
-
-        cross = lax.fori_loop(0, reach, cross_block, jnp.zeros((8 * count, 8 * part), f32))
-        share = share + collect(cross, 8 * count + 8 * begin)
+        sums = [[None, None] for _ in range(count)]
+        for x in range(reach):
+            from_high = [
+                along_x(lambda p: xhi3[2 * c + j, p - size_x] if p >= size_x else None, size_x - reach + x)
+                for j in range(2)
+            ]
+            from_low = [along_x(lambda p: xlo3[2 * c + j, reach + p] if p < 0 else None, x) for j in range(2)]
+            for near, layer, begin in ((from_high, size_x - reach + x, 0), (from_low, x, half)):
+                for tile in range(0, half, 8):
+                    for i in range(count):
+                        mine = out_ref[i, layer, begin + tile : begin + tile + 8, :]
+                        for j in range(2):
+                            term = mine * near[j][tile : tile + 8]
+                            sums[i][j] = term if sums[i][j] is None else sums[i][j] + term
+        rows = jnp.concatenate(
+            [jnp.concatenate([sums[i][j][None] for i in range(count)], axis=0).sum(axis=1) for j in range(2)], axis=0
+        )
+        rows = added_up(dot(three_parts(rows), jnp.ones((size_z, 128), bf16)), 2 * count)
+        lane = lax.broadcasted_iota(jnp.int32, (count, 128), 1)
+        for j in range(2):
+            share = share + jnp.where(lane == count + 2 * c + j, 2.0 * rows[j * count : (j + 1) * count], 0.0)
+        return share
+
+    share = lax.fori_loop(0, pairs, add_cross, share)
+    share = share[0:8] + pltpu.roll(share[8:16], 64, 1)
 
     stages = (
         (near, sum_one, me["gy"] * 2 + inner_z),
@@ -384,10 +401,7 @@
             shares = [shares[i] + shares[i + 1] for i in range(0, len(shares), 2)]
         share = shares[0]
 
-    share = share * scale
-    turned = share.T
-    gram_ref[...] = share[:, 0:count]
-    proj_ref[...] = 0.5 * (share[:, count : 2 * count] + turned[count : 2 * count, :])
+    sum_ref[...] = share * scale
 
     whole = pl.ds(0, count)
     for e, field in enumerate((o_hbm, first_ref, out_ref)):
@@ -397,26 +411,39 @@
         copy.wait_send()
 
 
+def finish(out_ref, sum_ref, out_hbm, gram_hbm, proj_hbm, gram_ref, proj_ref, sems):
+    move = pltpu.make_async_copy(out_ref, out_hbm, sems.at[0])
+    move.start()
+    total = jnp.concatenate([sum_ref[...], pltpu.roll(sum_ref[...], 64, 1)], axis=0)
+    turned = total.T
+    gram_ref[...] = total[:, 0:count]
+    proj_ref[...] = 0.5 * (total[:, count : 2 * count] + turned[count : 2 * count, :])
+    moves = [
+        move,
+        pltpu.make_async_copy(gram_ref, gram_hbm, sems.at[1]),
+        pltpu.make_async_copy(proj_ref, proj_hbm, sems.at[2]),
+    ]
+    for later in moves[1:]:
+        later.start()
+    for each in moves:
+        each.wait()
+
+
 def shards(orbitals, potential):
     sizes = [lax.axis_size(a) for a in axes]
     total = cells * size_z * sizes[0] * sizes[1] * sizes[2]
-    whole = pl.BlockSpec(memory_space=pltpu.VMEM)
     operands = (orbitals, potential, *(jnp.asarray(c) for c in constants()))
     vmem = lambda *shape: pltpu.VMEM(shape, f32)
-    return pl.pallas_call(
+    whole, anywhere = pl.BlockSpec(memory_space=pltpu.VMEM), pl.BlockSpec(memory_space=pltpu.HBM)
+    filtered, sums = pl.pallas_call(
         functools.partial(kernel, 1.0 / total),
-        out_shape=(
-            vmem(*orbitals.shape),
-            vmem(count, count),
-            vmem(count, count),
-        ),
-        in_specs=[pl.BlockSpec(memory_space=pltpu.HBM)] * len(operands),
-        out_specs=(whole, whole, whole),
+        out_shape=(vmem(*orbitals.shape), vmem(8, 128)),
+        in_specs=[anywhere] * len(operands),
+        out_specs=(whole, whole),
         scratch_shapes=[
             *(pltpu.VMEM(x.shape, x.dtype) for x in operands),
             vmem(count, size_x, size_y, size_z),
             vmem(count, size_x, size_y, size_z),
-            vmem(count, reach, size_y, size_z),
             vmem(2, count, reach, size_y, size_z),
             vmem(2, count, reach, size_y, size_z),
             vmem(count, reach, half, size_z),
@@ -427,8 +454,8 @@
             vmem(3, count, size_x * reach, size_z),
             vmem(3, pairs, 4 * reach, cells),
             vmem(3, pairs, 4 * reach, cells),
-            vmem(sizes[1] * 2, count, 128),
-            vmem(sizes[0] * sizes[2] // 2, count, 128),
+            vmem(sizes[1] * 2, 8, 128),
+            vmem(sizes[0] * sizes[2] // 2, 8, 128),
             pltpu.SemaphoreType.DMA((len(operands),)),
             pltpu.SemaphoreType.DMA((3, 6)),
             pltpu.SemaphoreType.DMA((3, 6, pairs)),
@@ -439,6 +466,18 @@
             collective_id=0, has_side_effects=True, vmem_limit_bytes=48 << 20
         ),
     )(*(pltpu.with_memory_space_constraint(x, pltpu.HBM) for x in operands))
+    return pl.pallas_call(
+        finish,
+        out_shape=(
+            jax.ShapeDtypeStruct(orbitals.shape, f32),
+            jax.ShapeDtypeStruct((count, count), f32),
+            jax.ShapeDtypeStruct((count, count), f32),
+        ),
+        in_specs=[whole, whole],
+        out_specs=(anywhere, anywhere, anywhere),
+        scratch_shapes=[vmem(count, count), vmem(count, count), pltpu.SemaphoreType.DMA((3,))],
+        compiler_params=pltpu.CompilerParams(vmem_limit_bytes=8 << 20),
+    )(pltpu.with_memory_space_constraint(filtered, pltpu.VMEM), pltpu.with_memory_space_constraint(sums, pltpu.VMEM))
 
 
 def solution(mesh):

time: 81.4 us -> 79.7 us (0.979)
  local copies, waits for them, and re-layouts: 2.52 us -> 0 us
  Pallas kernels: 78.1 us -> 79 us
    unnamed x3 -> x0, local copies, waits for them, and re-layouts: 2.52 us -> none
    pallas_call x0 -> x1, Pallas kernels: none -> 1.35 us  [shards(): pl.pallas_call(finish, out_shape=(jax.ShapeDtypeStruct(orbitals.shape, f3...]
where the time goes in v3:
time: 79.7 us; the launch traced here: 79.6 us
  Pallas kernels  79 us (99%)
    pallas_call x1, Pallas kernels, shards(): pl.pallas_call(functools.partial(kernel, 1.0 / total), out_shape=(vmem(*o...  77.6 us

profile of v3, /device:TPU:1, one launch (start us, length us, event | category | flops | bytes accessed | tf_op | source)
XLA Modules:
  0.0 79.6 jit_solution(9638608394517989108)
XLA Ops:
  0.6 77.6 %shard_map.103 = (f32[16,8,32,128]{3,2,1,0:T(8,128)S(1)}, f32[8,128]{1,0:T(8,128)S(1)}) custom-call(f32[16,8,32,128]{3,2,1,0:T(8,128)} %o_hbm.1, f32[8,32,128]{2,1,0:T(8,128)} %v_hbm.1, bf16[256,768]{1,0:T(8,128)(2,1)} %constant.12.clone.ay_hbm, bf16[256,192]{1,0:T(8,128)(2,1)} %constant.13.clone.fy_hbm, bf16[384,128]{1,0:T(8,128)(2,1)} %constant.14.clone.az_hbm, ...), custom_call_target="tpu_custom_call" | custom-call | tf_op jit(solution)/shard_map/pallas_call | solution.py:438
  78.3 1.4 %shard_map.104 = (f32[16,8,32,128]{3,2,1,0:T(8,128)}, f32[16,16]{1,0:T(8,128)}, f32[16,16]{1,0:T(8,128)}) custom-call(f32[16,8,32,128]{3,2,1,0:T(8,128)S(1)} %get-tuple-element.5.out_ref, f32[8,128]{1,0:T(8,128)S(1)} %get-tuple-element.6.sum_ref), custom_call_target="tpu_custom_call" | custom-call | tf_op jit(solution)/shard_map/pallas_call | solution.py:469

commit v4 on v3

--- a/solution.py
+++ b/solution.py
@@ -94,17 +94,14 @@
     out_ref, sum_ref,
     o_ref, v_ref, ay_ref, fy_ref, az_ref, cz_ref, pick_ref, gather_ref,
     first_ref, image_ref, xlo, xhi, xlo3, xhi3, ylo, yhi, ysl, ysh, zr, zs, sum_one, sum_two,
-    load_sem, send_sem, recv_sem, sum_send, sum_recv,
+    pair_sem, load_sem, send_sem, recv_sem, sum_send, sum_recv,
 ):
-    loads = [
-        pltpu.make_async_copy(src, dst, load_sem.at[i])
-        for i, (src, dst) in enumerate((
-            (o_hbm, o_ref), (pick_hbm, pick_ref), (v_hbm, v_ref), (ay_hbm, ay_ref), (fy_hbm, fy_ref),
-            (az_hbm, az_ref), (cz_hbm, cz_ref), (gather_hbm, gather_ref),
-        ))
-    ]
-    for load in loads:
-        load.start()
+    def load_pair(c):
+        return pltpu.make_async_copy(o_hbm.at[pl.ds(2 * c, 2)], o_ref.at[pl.ds(2 * c, 2)], pair_sem.at[c])
+
+    for c in range(pairs):
+        load_pair(c).start()
+
     sizes = {a: lax.axis_size(a) for a in axes}
     me = {a: lax.axis_index(a) for a in axes}
     right = {a: lax.rem(me[a] + 1, sizes[a]) for a in axes}
@@ -249,19 +246,28 @@
         lax.fori_loop(0, pairs, lambda c, carry: (body(c), carry)[1], 0)
 
     def start_first(c):
-        for copy in x_copies(0, o_hbm, pair(c), c):
+        load_pair(c).wait()
+        for copy in x_copies(0, o_ref, pair(c), c):
             copy.start()
 
     each(start_first)
-    for load in loads[:2]:
-        load.wait()
+    loads = [
+        pltpu.make_async_copy(src, dst, load_sem.at[i])
+        for i, (src, dst) in enumerate((
+            (pick_hbm, pick_ref), (v_hbm, v_ref), (ay_hbm, ay_ref), (fy_hbm, fy_ref),
+            (az_hbm, az_ref), (cz_hbm, cz_ref), (gather_hbm, gather_ref),
+        ))
+    ]
+    for load in loads:
+        load.start()
+    loads[0].wait()
     each(functools.partial(pack_send, 0, o_ref))
-    for load in loads[2:]:
+    for load in loads[1:]:
         load.wait()
 
     def step_one(c):
         wait_yz(0, c)
-        wait_x(0, o_hbm, c)
+        wait_x(0, o_ref, c)
 
         def write(o, x, value):
             first_ref[o, x] = value * (sigma_one / spread)
@@ -298,13 +304,17 @@
             for x in range(size_x):
                 image_ref[o, x] += around[x * size_y : (x + 1) * size_y, i * size_z : (i + 1) * size_z]
 
+    lag = 3
+
     def step_two_and_faces(c):
         step_two(c)
-        add_faces(c - 1)
-
-    step_two(0)
-    lax.fori_loop(1, pairs, lambda c, carry: (step_two_and_faces(c), carry)[1], 0)
-    add_faces(pairs - 1)
+
+        @pl.when(c >= lag)
+        def _():
+            add_faces(c - lag)
+
+    each(step_two_and_faces)
+    lax.fori_loop(pairs - lag, pairs, lambda c, carry: (add_faces(c), carry)[1], 0)
 
     def block(ref, x, tile):
         return split(ref[:, x, tile * 8 : (tile + 1) * 8, :].reshape(8 * count, size_z))
@@ -404,7 +414,7 @@
     sum_ref[...] = share * scale
 
     whole = pl.ds(0, count)
-    for e, field in enumerate((o_hbm, first_ref, out_ref)):
+    for e, field in enumerate((o_ref, first_ref, out_ref)):
         for copy in x_copies(e, field, whole, 0) + yz_copies(e, whole, pl.ds(0, pairs), 0):
             copy.wait_send()
     for copy in sent:
@@ -456,7 +466,8 @@
             vmem(3, pairs, 4 * reach, cells),
             vmem(sizes[1] * 2, 8, 128),
             vmem(sizes[0] * sizes[2] // 2, 8, 128),
-            pltpu.SemaphoreType.DMA((len(operands),)),
+            pltpu.SemaphoreType.DMA((pairs,)),
+            pltpu.SemaphoreType.DMA((len(operands) - 1,)),
             pltpu.SemaphoreType.DMA((3, 6)),
             pltpu.SemaphoreType.DMA((3, 6, pairs)),
             pltpu.SemaphoreType.DMA((2,)),

time: 79.7 us -> 79.3 us (level)
  no operation moved by 1% of the time
where the time goes in v4:
time: 79.3 us; the launch traced here: 79.1 us
  Pallas kernels  78.4 us (99%)
    pallas_call x1, Pallas kernels, shards(): pl.pallas_call(functools.partial(kernel, 1.0 / total), out_shape=(vmem(*o...  77.1 us

profile of v4, /device:TPU:1, one launch (start us, length us, event | category | flops | bytes accessed | tf_op | source)
XLA Modules:
  0.0 79.1 jit_solution(9050482951624662511)
XLA Ops:
  0.6 77.1 %shard_map.103 = (f32[16,8,32,128]{3,2,1,0:T(8,128)S(1)}, f32[8,128]{1,0:T(8,128)S(1)}) custom-call(f32[16,8,32,128]{3,2,1,0:T(8,128)} %o_hbm.1, f32[8,32,128]{2,1,0:T(8,128)} %v_hbm.1, bf16[256,768]{1,0:T(8,128)(2,1)} %constant.12.clone.ay_hbm, bf16[256,192]{1,0:T(8,128)(2,1)} %constant.13.clone.fy_hbm, bf16[384,128]{1,0:T(8,128)(2,1)} %constant.14.clone.az_hbm, ...), custom_call_target="tpu_custom_call" | custom-call | tf_op jit(solution)/shard_map/pallas_call | solution.py:448
  77.7 1.4 %shard_map.104 = (f32[16,8,32,128]{3,2,1,0:T(8,128)}, f32[16,16]{1,0:T(8,128)}, f32[16,16]{1,0:T(8,128)}) custom-call(f32[16,8,32,128]{3,2,1,0:T(8,128)S(1)} %get-tuple-element.5.out_ref, f32[8,128]{1,0:T(8,128)S(1)} %get-tuple-element.6.sum_ref), custom_call_target="tpu_custom_call" | custom-call | tf_op jit(solution)/shard_map/pallas_call | solution.py:480

commit v5 on v4

--- a/solution.py
+++ b/solution.py
@@ -360,7 +360,6 @@
     share = collect(inner)
 
     def add_cross(c, share):
-        wait_x(2, out_ref, c)
         sums = [[None, None] for _ in range(count)]
         for x in range(reach):
             from_high = [
@@ -384,7 +383,12 @@
             share = share + jnp.where(lane == count + 2 * c + j, 2.0 * rows[j * count : (j + 1) * count], 0.0)
         return share
 
-    share = lax.fori_loop(0, pairs, add_cross, share)
+    def two_crosses(c, share):
+        wait_x(2, out_ref, 2 * c)
+        wait_x(2, out_ref, 2 * c + 1)
+        return add_cross(2 * c + 1, add_cross(2 * c, share))
+
+    share = lax.fori_loop(0, pairs // 2, two_crosses, share)
     share = share[0:8] + pltpu.roll(share[8:16], 64, 1)
 
     stages = (

time: 79.3 us -> 79.1 us (level)
  no operation moved by 1% of the time
where the time goes in v5:
time: 79.1 us; the launch traced here: 78.9 us
  Pallas kernels  78.3 us (99%)
    pallas_call x1, Pallas kernels, shards(): pl.pallas_call(functools.partial(kernel, 1.0 / total), out_shape=(vmem(*o...  76.9 us

profile of v5, /device:TPU:1, one launch (start us, length us, event | category | flops | bytes accessed | tf_op | source)
XLA Modules:
  0.0 78.9 jit_solution(344787706453997501)
XLA Ops:
  0.6 76.9 %shard_map.103 = (f32[16,8,32,128]{3,2,1,0:T(8,128)S(1)}, f32[8,128]{1,0:T(8,128)S(1)}) custom-call(f32[16,8,32,128]{3,2,1,0:T(8,128)} %o_hbm.1, f32[8,32,128]{2,1,0:T(8,128)} %v_hbm.1, bf16[256,768]{1,0:T(8,128)(2,1)} %constant.12.clone.ay_hbm, bf16[256,192]{1,0:T(8,128)(2,1)} %constant.13.clone.fy_hbm, bf16[384,128]{1,0:T(8,128)(2,1)} %constant.14.clone.az_hbm, ...), custom_call_target="tpu_custom_call" | custom-call | tf_op jit(solution)/shard_map/pallas_call | solution.py:452
  77.5 1.4 %shard_map.104 = (f32[16,8,32,128]{3,2,1,0:T(8,128)}, f32[16,16]{1,0:T(8,128)}, f32[16,16]{1,0:T(8,128)}) custom-call(f32[16,8,32,128]{3,2,1,0:T(8,128)S(1)} %get-tuple-element.5.out_ref, f32[8,128]{1,0:T(8,128)S(1)} %get-tuple-element.6.sum_ref), custom_call_target="tpu_custom_call" | custom-call | tf_op jit(solution)/shard_map/pallas_call | solution.py:484
